TPU v7x, 32 devices: a whole 2x2x4 slice. The times are simulated.
32 devices in a mesh: lat: 4 (over x, core), lon: 8 (over z, y).
Axes of the slice: x: 2, y: 2, z: 4, core: 2. Of those that a mesh axis runs over, the one named last changes fastest.
Arguments:
- grad_out: bfloat16 [704, 1440, 256], P('lat', 'lon'), may hold values from -6 to 6
- block_input: bfloat16 [704, 1440, 256], P('lat', 'lon'), may hold values from -6 to 6
- leg_table: bfloat16 [384, 384, 704], P('lat'), may hold values from -1 to 1, as said below
- spec_coeff: bfloat16 [384, 384, 2, 256], P(None, 'lat', None, 'lon'), may hold values from -6 to 6
- spec_filter: float32 [384, 256], P(None, 'lon'), may hold values from -6 to 6
- cycle_weight: float32 [704, 3], replicated, may hold values from 0.2 to 2
- cycle_shift: int32 [704, 3], replicated, may hold values from -1 to 1
- tap_weight: bfloat16 [3, 256, 256], replicated, may hold values from -0.21875 to 0.21875
Outputs:
- spec_grad: bfloat16 [384, 384, 2, 256], P(None, 'lat', None, 'lon')
- filter_grad: float32 [384, 256], P(None, 'lon')
- input_grad: bfloat16 [704, 1440, 256], P('lat', 'lon')
- taps_grad: float32 [3, 256, 256], replicated
Inputs may be any that keep to these rules, and one draw needn't show every extreme that they name: `leg_table`: zero wherever the degree l is below the order m.
All inputs are finite; a program needn't handle non-finite values.
Results may differ from a plain program's by a relative error of at most 0.013.
Values may be sent and summed in bfloat16 or wider, within the bound.
A program may use at most 320 MiB of HBM per device.

v0:
```python
import math

import jax
import jax.numpy as jnp
from jax import lax
from jax.sharding import PartitionSpec as P


def padded_2(shard, sides, width):
    for axis, dim in sides:
        size, length = (lax.axis_size(axis), shard.shape[dim])
        up = [(i, (i + 1) % size) for i in range(size)]
        down = [(j, i) for i, j in up]
        last = lax.slice_in_dim(shard, length - width, length, axis=dim)
        first = lax.slice_in_dim(shard, 0, width, axis=dim)
        before = lax.ppermute(last, axis, up)
        after = lax.ppermute(first, axis, down)
        shard = jnp.concatenate([before, shard, after], axis=dim)
    return shard


def fourier_table(lon_count, mode_count):
    longitude = jnp.arange(lon_count, dtype=jnp.int32)[:, None]
    orders = jnp.arange(mode_count, dtype=jnp.int32)[None, :]
    phase = (longitude * orders % lon_count).astype(jnp.float32) * (2.0 * math.pi / lon_count)
    table = jnp.stack([jnp.cos(phase), jnp.sin(phase)], axis=-1) / math.sqrt(lon_count)
    return table.astype(jnp.bfloat16)


def on_device(
    grad_out, block_input, leg_table, spec_coeff, spec_filter, cycle_weight, cycle_shift, tap_weight
):
    rows_here, lons_here, channels = grad_out.shape
    lon_total = lons_here * lax.axis_size("lon")
    cycle_total = rows_here * lax.axis_size("lat")
    order_total = leg_table.shape[0] * lax.axis_size("lat")
    table = fourier_table(lon_total, order_total)
    fourier = jnp.einsum(
        "opt,phu->tohu",
        lax.all_to_all(grad_out, "lon", split_axis=2, concat_axis=1, tiled=True),
        table,
        preferred_element_type=jnp.float32,
    ).astype(jnp.bfloat16)
    degree = jnp.einsum(
        "mla,camr->lmrc",
        leg_table,
        lax.all_to_all(fourier, "lat", split_axis=2, concat_axis=1, tiled=True),
        preferred_element_type=jnp.float32,
    )
    spec_grad = (degree * spec_filter[:, None, None, :]).astype(jnp.bfloat16)
    filter_part = jnp.sum(spec_coeff.astype(jnp.float32) * degree, axis=(1, 2)) / math.sqrt(
        2 * order_total
    )
    padded = padded_2(grad_out, (("lat", 0), ("lon", 1)), 1)
    cycle_start = lax.axis_index("lat") * rows_here
    weight_pad = jnp.pad(cycle_weight, ((1, 1), (0, 0)))
    shift_pad = jnp.pad(cycle_shift, ((1, 1), (0, 0)))
    flat_input = block_input.reshape(-1, channels)
    local_grad = jnp.zeros((rows_here * lons_here, channels), jnp.float32)
    partials = []
    for tap_index, offset in enumerate((-1, 0, 1)):
        source = padded[1 - offset : 1 - offset + rows_here]
        coef = lax.dynamic_slice_in_dim(weight_pad, cycle_start + 1 - offset, rows_here, 0)[
            :, tap_index
        ]
        shifts = lax.dynamic_slice_in_dim(shift_pad, cycle_start + 1 - offset, rows_here, 0)[
            :, tap_index
        ]
        picked = jnp.zeros((rows_here, lons_here, channels), jnp.float32)
        for column_shift in (-1, 0, 1):
            window = source[:, 1 - column_shift : 1 - column_shift + lons_here].astype(jnp.float32)
            picked = picked + (shifts == column_shift).astype(jnp.float32)[:, None, None] * window
        spread = (coef[:, None, None] * picked).astype(jnp.bfloat16).reshape(-1, channels)
        local_grad = local_grad + lax.dot_general(
            spread,
            tap_weight[tap_index],
            (((1,), (1,)), ((), ())),
            preferred_element_type=jnp.float32,
        )
        partials.append(
            lax.dot_general(
                flat_input, spread, (((0,), (0,)), ((), ())), preferred_element_type=jnp.float32
            )
        )
    taps_part = jnp.stack(partials) / math.sqrt(cycle_total * lon_total)
    input_grad = local_grad.reshape(rows_here, lons_here, channels).astype(jnp.bfloat16)
    taps_grad = lax.psum(taps_part, ("lat", "lon"))
    filter_grad = lax.psum(filter_part, "lat")
    return (spec_grad, filter_grad, input_grad, taps_grad)


def solution(mesh):
    in_specs = (
        P("lat", "lon", None),
        P("lat", "lon", None),
        P("lat", None, None),
        P(None, "lat", None, "lon"),
        P(None, "lon"),
        P(),
        P(),
        P(),
    )
    out_specs = (P(None, "lat", None, "lon"), P(None, "lon"), P("lat", "lon", None), P())
    return jax.shard_map(
        on_device, mesh=mesh, in_specs=in_specs, out_specs=out_specs, check_vma=False
    )
```

profile of v0, /device:TPU:12, one launch (start us, length us, event | category | flops | bytes accessed | tf_op | source)
XLA Modules:
  0.0 1133.0 jit_solution(408140294293342798)
XLA Ops:
  7.2 33.5 %copy.37 = bf16[176,180,256]{1,0,2:T(8,128)(2,1)} copy(bf16[176,180,256]{2,0,1:T(8,128)(2,1)} %param.8) | data formatting | bytes 32440320 | tf_op args[0]
  40.7 6.4 all-to-all-start
  50.6 10.1 fusion.13
  62.7 2.4 collective-permute-start.3
  65.2 481.0 %collective-permute-done.2 = bf16[178,1,256]{2,0,1:T(8,128)(2,1)S(1)} collective-permute-done((bf16[178,1,256]{2,0,1:T(8,128)(2,1)S(1)}, bf16[178,1,256]{2,0,1:T(8,128)(2,1)S(1)}, u32[]{:S(2)}, u32[]{:S(2)}) %collective-permute-start.2) | collective-permute-done | bytes 91168 | tf_op jit(solution)/shard_map/ppermute | solution.py:17
  546.2 31.0 %pad_maximum_fusion = (bf16[178,181,256]{2,0,1:T(8,128)(2,1)}, bf16[178,181,256]{2,0,1:T(8,128)(2,1)}) fusion(bf16[178,1,256]{2,0,1:T(8,128)(2,1)S(1)} %collective-permute-done.2, bf16[1,180,256]{2,0,1:T(2,128)(2,1)S(1)} %copy.46, bf16[176,180,256]{2,0,1:T(8,128)(2,1)} %param.8, bf16[1,180,256]{2,0,1:T(2,128)(2,1)S(1)} %copy.45, ...), kind=kLoop, calls=%fused_computation.8 | loop fusion | flops 131964928 | bytes 49577984 | tf_op jit(solution)/shard_map/concatenate | solution.py:18
  577.3 29.8 %multiply_convert_fusion.2 = bf16[176,180,256]{2,0,1:T(8,128)(2,1)S(1)} fusion(bf16[178,181,256]{2,0,1:T(8,128)(2,1)} %get-tuple-element.25, bf16[1,180,256]{2,0,1:T(2,128)(2,1)S(1)} %copy.46, bf16[176,180,256]{2,0,1:T(8,128)(2,1)} %param.8, bf16[178,181,256]{2,0,1:T(8,128)(2,1)} %get-tuple-element.24, f32[176]{0:T(256)S(1)} %bitcast.94, f32[176]{0:T(256)S(1)} %bitcast.93, ...), kind=kLoop, calls=%fused_computation.7 | loop fusion | flops 105431040 | bytes 64975616 | tf_op jit(solution)/shard_map/convert_element_type | solution.py:73
  607.1 6.0 copy-done.1
  613.0 12.9 %copy.48 = bf16[176,180,256]{2,1,0:T(8,128)(2,1)} copy(bf16[176,180,256]{2,0,1:T(8,128)(2,1)S(1)} %multiply_convert_fusion.2) | data formatting | bytes 32440320 | tf_op jit(solution)/shard_map/convert_element_type | solution.py:73
  626.0 15.5 %convolution_bitcast_fusion.2 = f32[1,256,256]{1,2,0:T(8,128)} fusion(bf16[176,180,256]{2,0,1:T(8,128)(2,1)} %copy-done.1, bf16[176,180,256]{2,0,1:T(8,128)(2,1)} %param.9), kind=kOutput, calls=%fused_computation.32 | convolution fusion | flops 4152360960 | bytes 32702464 | tf_op jit(solution)/shard_map/dot_general | solution.py:81
  641.5 43.0 %multiply_convert_fusion = (bf16[176,180,256]{2,0,1:T(8,128)(2,1)}, bf16[176,180,256]{2,0,1:T(8,128)(2,1)}) fusion(bf16[178,181,256]{2,0,1:T(8,128)(2,1)} %get-tuple-element.25, bf16[176,180,256]{2,0,1:T(8,128)(2,1)S(1)} %bitcast.83, bf16[1,180,256]{2,0,1:T(2,128)(2,1)} %copy-done.2, bf16[178,181,256]{2,0,1:T(8,128)(2,1)} %get-tuple-element.24, ...), kind=kLoop, calls=%fused_computation.5 | loop fusion | flops 186531840 | bytes 113638912 | tf_op jit(solution)/shard_map/convert_element_type | solution.py:73
  684.5 15.5 %convolution_bitcast_fusion = f32[1,256,256]{1,2,0:T(8,128)} fusion(bf16[176,180,256]{2,0,1:T(8,128)(2,1)} %get-tuple-element.22, bf16[176,180,256]{2,0,1:T(8,128)(2,1)} %param.9), kind=kOutput, calls=%fused_computation.30 | convolution fusion | flops 4152360960 | bytes 32702464 | tf_op jit(solution)/shard_map/dot_general | solution.py:81
  700.0 8.7 convolution_bitcast_fusion.1
  710.8 22.3 %reshape.167 = bf16[31680,256]{1,0:T(8,128)(2,1)} reshape(bf16[176,180,256]{2,1,0:T(8,128)(2,1)} %copy.48) | data formatting | bytes 32440320 | tf_op jit(solution)/shard_map/reshape | solution.py:73
  733.1 41.1 %copy.39 = bf16[176,8,180,32]{2,1,0,3:T(8,128)(2,1)} copy(bf16[176,8,180,32]{2,0,3,1:T(8,128)(2,1)} %bitcast.4) | data formatting | bytes 32440320 | tf_op jit(solution)/shard_map/all_to_all | solution.py:40
  774.2 37.8 %reshape.180 = bf16[176,1440,32,1]{1,0,2,3:T(8,128)(2,1)} reshape(bf16[176,8,180,32]{2,1,0,3:T(8,128)(2,1)} %copy.39) | data formatting | bytes 32440320 | tf_op jit(solution)/shard_map/all_to_all | solution.py:40
  811.9 20.1 %convert_bitcast_fusion = bf16[32,176,384,2]{2,1,0,3:T(8,128)(2,1)} fusion(bf16[176,1440,32,1]{1,0,2,3:T(8,128)(2,1)} %reshape.180, f32[1440,384,1]{1,0,2:T(8,128)S(1)} %copy-done.3, f32[1440,384,1]{1,0,2:T(8,128)} %get-tuple-element.46), kind=kOutput, calls=%fused_computation.16 | convolution fusion | flops 12464726016 | bytes 29294592 | tf_op jit(solution)/shard_map/opt,phu->tohu/dot_general | solution.py:38
  832.0 17.1 %copy.40 = bf16[32,176,384,2]{1,0,3,2:T(8,128)(2,1)} copy(bf16[32,176,384,2]{2,1,0,3:T(8,128)(2,1)} %convert_bitcast_fusion) | data formatting | bytes 17301504 | tf_op jit(solution)/shard_map/convert_element_type | solution.py:43
  849.1 6.6 all-to-all-start.1
  855.8 20.7 %fusion.18 = f32[31680,256]{1,0:T(8,128)} fusion(bf16[31680,256]{1,0:T(8,128)(2,1)} %reshape.167, bf16[3,256,256]{2,1,0:T(8,128)(2,1)S(1)} %copy-done.5), kind=kOutput, calls=%fused_computation.36 | convolution fusion | flops 4152360960 | bytes 48791552 | tf_op jit(solution)/shard_map/dot_general | solution.py:74
  876.5 19.0 %copy.49 = bf16[176,180,256]{2,1,0:T(8,128)(2,1)} copy(bf16[176,180,256]{2,0,1:T(8,128)(2,1)} %get-tuple-element.23) | data formatting | bytes 32440320 | tf_op jit(solution)/shard_map/convert_element_type | solution.py:73
  895.5 19.0 %copy.51 = bf16[176,180,256]{2,1,0:T(8,128)(2,1)} copy(bf16[176,180,256]{2,0,1:T(8,128)(2,1)} %get-tuple-element.22) | data formatting | bytes 32440320 | tf_op jit(solution)/shard_map/convert_element_type | solution.py:73
  914.5 22.2 %reshape.168 = bf16[31680,256]{1,0:T(8,128)(2,1)} reshape(bf16[176,180,256]{2,1,0:T(8,128)(2,1)} %copy.49) | data formatting | bytes 32440320 | tf_op jit(solution)/shard_map/reshape | solution.py:73
  936.7 22.3 %reshape.169 = bf16[31680,256]{1,0:T(8,128)(2,1)} reshape(bf16[176,180,256]{2,1,0:T(8,128)(2,1)} %copy.51) | data formatting | bytes 32440320 | tf_op jit(solution)/shard_map/reshape | solution.py:73
  959.0 28.3 %convolution_add_fusion.1 = f32[31680,256]{1,0:T(8,128)} fusion(f32[31680,256]{1,0:T(8,128)} %fusion.18, bf16[31680,256]{1,0:T(8,128)(2,1)} %reshape.168, bf16[3,256,256]{2,1,0:T(8,128)(2,1)S(1)} %copy-done.5), kind=kOutput, calls=%fused_computation.3 | convolution fusion | flops 4160471040 | bytes 81231872 | tf_op jit(solution)/shard_map/dot_general | solution.py:74
  987.3 22.8 %fusion.2 = bf16[31680,256]{1,0:T(8,128)(2,1)} fusion(f32[31680,256]{1,0:T(8,128)} %convolution_add_fusion.1, bf16[31680,256]{1,0:T(8,128)(2,1)} %reshape.169, bf16[3,256,256]{2,1,0:T(8,128)(2,1)S(1)} %copy-done.5), kind=kOutput, calls=%fused_computation.4 | convolution fusion | flops 4168581120 | bytes 65011712 | tf_op jit(solution)/shard_map/dot_general | solution.py:74
  1010.1 22.2 %convert_element_type.202 = bf16[176,180,256]{2,1,0:T(8,128)(2,1)} reshape(bf16[31680,256]{1,0:T(8,128)(2,1)} %fusion.2) | data formatting | bytes 32440320 | tf_op jit(solution)/shard_map/convert_element_type | solution.py:86
  1032.4 19.3 %copy.52 = bf16[176,180,256]{2,0,1:T(8,128)(2,1)} copy(bf16[176,180,256]{2,1,0:T(8,128)(2,1)} %convert_element_type.202) | data formatting | bytes 32440320
  1053.9 17.7 %copy.41 = bf16[32,176,4,96,2]{3,1,2,4,0:T(8,128)(2,1)} copy(bf16[32,176,4,96,2]{1,0,4,3,2:T(8,128)(2,1)} %bitcast.6) | data formatting | bytes 17301504 | tf_op jit(solution)/shard_map/all_to_all | solution.py:47
  1071.6 15.7 %copy.42 = bf16[32,704,96,2]{1,0,3,2:T(8,128)(2,1)} copy(bf16[32,704,96,2]{2,1,3,0:T(8,128)(2,1)} %bitcast.84) | data formatting | bytes 17301504 | tf_op jit(solution)/shard_map/all_to_all | solution.py:47
  1087.3 25.6 %fusion.4 = (f32[384,32]{0,1:T(8,128)S(1)}, bf16[384,96,2,32]{0,3,2,1:T(8,128)(2,1)}) fusion(bf16[384,96,2,32]{0,3,2,1:T(8,128)(2,1)} %param.11, f32[384,32]{0,1:T(8,128)S(1)} %copy-done.4, bf16[32,704,96,2]{1,0,3,2:T(8,128)(2,1)} %copy.42, bf16[96,384,704]{1,2,0:T(8,128)(2,1)} %param.10), kind=kOutput, calls=%fused_computation.15 | convolution fusion | flops 3333672960 | bytes 70090752 | tf_op jit(solution)/shard_map/mla,camr->lmrc/dot_general | solution.py:44
  1112.9 12.8 %psum.14 = f32[384,32]{0,1:T(8,128)} all-reduce(f32[384,32]{0,1:T(8,128)S(1)} %broadcast_multiply_fusion), channel_id=1, replica_groups=mesh['lat'=4,'lon'=8] {'lat'}, use_global_device_ids=true, to_apply=%region_1.2 | all-reduce | flops 12288 | bytes 98304 | tf_op jit(solution)/shard_map/psum | solution.py:88
  (48 shorter events, 9.9 us)
Async XLA Ops:
  40.7 9.2 copy-start.7
  40.7 692.4 %all-to-all-start = ((bf16[176,180,256]{1,0,2:T(8,128)(2,1)}), bf16[176,180,256]{1,0,2:T(8,128)(2,1)}, u32[]{:S(2)}, u32[]{:S(2)}) async-start(bf16[176,180,256]{1,0,2:T(8,128)(2,1)} %copy.37), calls=%async_computation | async-start | bytes 46137344 | tf_op jit(solution)/shard_map/all_to_all | solution.py:40
  47.1 18.0 %copy-start.6 = (f32[704,3]{0,1:T(4,128)S(1)}, f32[704,3]{0,1:T(4,128)}, u32[]{:S(2)}) copy-start(f32[704,3]{0,1:T(4,128)} %param.13) | copy-start | bytes 25348
  47.1 1004.5 %all-reduce.4.cloned.1.call-start = ((), (), s32[]{:S(2)}) async-start(), calls=%async_computation.2 | async-start | bytes 1572864 | tf_op jit(solution)/shard_map/psum | solution.py:87
  48.8 11.9 %collective-permute-start.1 = (bf16[1,180,256]{2,1,0:T(8,128)(2,1)S(1)}, bf16[1,180,256]{2,1,0:T(8,128)(2,1)S(1)}, u32[]{:S(2)}, u32[]{:S(2)}) collective-permute-start(bf16[1,180,256]{2,1,0:T(8,128)(2,1)S(1)} %copy.58), channel_id=1, source_target_pairs={{8,0},{16,8},{24,16},{0,24},{9,1},{17,9},{25,17},{1,25},{10,2},{18... | collective-permute-start | bytes 276488 | tf_op jit(solution)/shard_map/ppermute | solution.py:17
  49.8 11.0 collective-permute-start
  61.0 516.2 %copy-start.2 = (bf16[1,180,256]{2,0,1:T(2,128)(2,1)}, bf16[1,180,256]{2,0,1:T(2,128)(2,1)S(1)}, u32[]{:S(2)}) copy-start(bf16[1,180,256]{2,0,1:T(2,128)(2,1)S(1)} %copy.45) | copy-start | bytes 276484
  62.1 484.1 %collective-permute-start.2 = (bf16[178,1,256]{2,0,1:T(8,128)(2,1)S(1)}, bf16[178,1,256]{2,0,1:T(8,128)(2,1)S(1)}, u32[]{:S(2)}, u32[]{:S(2)}) collective-permute-start(bf16[178,1,256]{2,0,1:T(8,128)(2,1)S(1)} %get-tuple-element.26), channel_id=1, source_target_pairs={{1,0},{2,1},{3,2},{4,3},{5,4},{6,5},{7,6},{0,7},{9,8},{10,9},{11,1... | collective-permute-start | bytes 273416 | tf_op jit(solution)/shard_map/ppermute | solution.py:17
  62.7 483.6 %collective-permute-start.3 = (bf16[178,1,256]{2,0,1:T(8,128)(2,1)S(1)}, bf16[178,1,256]{2,0,1:T(8,128)(2,1)S(1)}, u32[]{:S(2)}, u32[]{:S(2)}) collective-permute-start(bf16[178,1,256]{2,0,1:T(8,128)(2,1)S(1)} %get-tuple-element.27), channel_id=1, source_target_pairs={{0,1},{1,2},{2,3},{3,4},{4,5},{5,6},{6,7},{7,0},{8,9},{9,10},{10,1... | collective-permute-start | bytes 273416 | tf_op jit(solution)/shard_map/ppermute | solution.py:16
  607.0 6.0 copy-start.1
  613.0 28.5 %slice-start = ((s8[16220160]{0:T(1024)(128)(4,1)}), s8[4194304]{0:T(1024)(128)(4,1)S(1)}, s32[]{:S(2)}) async-start(s8[16220160]{0:T(1024)(128)(4,1)} %bitcast.82), calls=%async_computation.3 | async-start | bytes 8388608
  613.0 28.5 %slice-start.1 = ((s8[16220160]{0:T(1024)(128)(4,1)}), s8[4194304]{0:T(1024)(128)(4,1)S(1)}, s32[]{:S(2)}) async-start(s8[16220160]{0:T(1024)(128)(4,1)} %bitcast.82), calls=%async_computation.4 | async-start | bytes 8388608
  626.0 15.5 %slice-start.2 = ((s8[16220160]{0:T(1024)(128)(4,1)}), s8[4194304]{0:T(1024)(128)(4,1)S(1)}, s32[]{:S(2)}) async-start(s8[16220160]{0:T(1024)(128)(4,1)} %bitcast.82), calls=%async_computation.5 | async-start | bytes 8388608
  626.0 15.5 %slice-start.3 = ((s8[16220160]{0:T(1024)(128)(4,1)}), s8[3637248]{0:T(1024)(128)(4,1)S(1)}, s32[]{:S(2)}) async-start(s8[16220160]{0:T(1024)(128)(4,1)} %bitcast.82), calls=%async_computation.6 | async-start | bytes 7274496
  684.5 15.5 %copy-start = (bf16[176,180,256]{2,0,1:T(8,128)(2,1)S(1)}, bf16[176,180,256]{2,0,1:T(8,128)(2,1)}, u32[]{:S(2)}) copy-start(bf16[176,180,256]{2,0,1:T(8,128)(2,1)} %get-tuple-element.23) | copy-start | bytes 48660484
  774.2 37.8 %copy-start.3 = (f32[1440,384,1]{1,0,2:T(8,128)S(1)}, f32[1440,384,1]{1,0,2:T(8,128)}, u32[]{:S(2)}) copy-start(f32[1440,384,1]{1,0,2:T(8,128)} %get-tuple-element.45) | copy-start | bytes 6635524
  849.1 6.7 copy-start.5
  849.1 204.8 %all-to-all-start.1 = ((bf16[32,176,384,2]{1,0,3,2:T(8,128)(2,1)}), bf16[32,176,384,2]{1,0,3,2:T(8,128)(2,1)}, u32[]{:S(2)}, u32[]{:S(2)}) async-start(bf16[32,176,384,2]{1,0,3,2:T(8,128)(2,1)} %copy.40), calls=%async_computation.1 | async-start | bytes 25165824 | tf_op jit(solution)/shard_map/all_to_all | solution.py:47
  1053.9 33.4 %copy-start.4 = (f32[384,32]{0,1:T(8,128)S(1)}, f32[384,32]{0,1:T(8,128)}, u32[]{:S(2)}) copy-start(f32[384,32]{0,1:T(8,128)} %param.12) | copy-start | bytes 147460
Sparse Core Ops, SparseCore 0:
  710.9 129.4 all-reduce.3
where the time goes:
time: 1150 us; the launch traced here: 1130 us
  waiting for transfers between devices  481 us (42%)
  local copies, waits for them, and re-layouts  332 us (29%)
  matrix products  157 us (14%)
  other arithmetic  118 us (10%)
  starting transfers between devices  17.1 us (1%)
  between operations  14.7 us (1%)
  blocking collectives  12.8 us (1%)
    ppermute x2, waiting for transfers between devices, padded_2(): after = lax.ppermute(first, axis, down)  481 us
    all_to_all x2, local copies, waits for them, and re-layouts, on_device(): lax.all_to_all(grad_out, 'lon', split_axis=2, concat_axis=1, tiled=True)  78.9 us
    convert_element_type x2, other arithmetic, on_device(): (coef[:, None, None] * picked).astype(jnp.bfloat16).reshape(-1, channels)  72.8 us
    dot_general x3, matrix products, on_device(): lax.dot_general(spread, tap_weight[tap_index], (((1,), (1,)), ((), ())),...  71.9 us
    reshape x3, local copies, waits for them, and re-layouts, on_device(): (coef[:, None, None] * picked).astype(jnp.bfloat16).reshape(-1, channels)  66.8 us
    unnamed x29, local copies, waits for them, and re-layouts  61.1 us
    convert_element_type x3, local copies, waits for them, and re-layouts, on_device(): (coef[:, None, None] * picked).astype(jnp.bfloat16).reshape(-1, channels)  50.9 us
    dot_general x3, matrix products, on_device(): lax.dot_general(flat_input, spread, (((0,), (0,)), ((), ())), preferred_e...  39.6 us
  transfers between devices with their start and end apart: 7, of which 1 were waited for; matrix products, arithmetic and copies ran while one was open for 45% of the time, Pallas kernels for 0%

commit v1 on v0

v1 whole, which is shorter than its diff:
```python
import functools
import math

import jax
import jax.numpy as jnp
from jax import lax
from jax.experimental import pallas as pl
from jax.experimental.pallas import tpu as pltpu
from jax.sharding import PartitionSpec as P

VMEM_BYTES = 48 * 2**20


def largest_divisor(number, most):
    return max(d for d in range(1, most + 1) if number % d == 0)


def split_table(sectors, lons_here, mode_count):
    shape = (sectors, 2 * mode_count, lons_here)
    lon = lax.broadcasted_iota(jnp.int32, shape, 0) * lons_here + lax.broadcasted_iota(
        jnp.int32, shape, 2
    )
    row = lax.broadcasted_iota(jnp.int32, shape, 1)
    lon_count = sectors * lons_here
    phase = (lon * (row // 2) % lon_count).astype(jnp.float32) * (2.0 * math.pi / lon_count)
    value = jnp.where(row % 2 == 0, jnp.cos(phase), jnp.sin(phase)) / math.sqrt(lon_count)
    return value.astype(jnp.bfloat16)


def pack_kernel(groups, lanes, x_ref, out_ref):
    packs = x_ref.shape[1]
    for j in range(groups):
        parts = [x_ref[0, q, 0, :, j * lanes : (j + 1) * lanes] for q in range(packs)]
        out_ref[j, 0] = jnp.concatenate(parts, axis=-1)


def pack(field, chunk, groups):
    _, packs, slots, lons, channels = field.shape
    lanes = channels // groups
    return pl.pallas_call(
        functools.partial(pack_kernel, groups, lanes),
        grid=(slots,),
        in_specs=[pl.BlockSpec((1, packs, 1, lons, channels), lambda s: (chunk, 0, s, 0, 0))],
        out_specs=pl.BlockSpec((groups, 1, lons, packs * lanes), lambda s: (0, s, 0, 0)),
        out_shape=jax.ShapeDtypeStruct((groups, slots, lons, packs * lanes), jnp.bfloat16),
        compiler_params=pltpu.CompilerParams(vmem_limit_bytes=VMEM_BYTES),
        cost_estimate=pl.CostEstimate(
            flops=0, bytes_accessed=4 * slots * packs * lons * channels, transcendentals=0
        ),
    )(field)


def analyse_kernel(table_ref, x_ref, out_ref):
    sectors, slots, _, width = x_ref.shape
    total = None
    for j in range(sectors):
        cells = jnp.concatenate([x_ref[j, s] for s in range(slots)], axis=-1)
        part = jnp.dot(table_ref[j], cells, preferred_element_type=jnp.float32)
        total = part if total is None else total + part
    for s in range(slots):
        out_ref[0, s] = total[:, s * width : (s + 1) * width].astype(jnp.bfloat16)


def analyse(table, cells, bands):
    sectors, slots, lons, width = cells.shape
    rows = table.shape[1] // bands
    return pl.pallas_call(
        analyse_kernel,
        grid=(bands,),
        in_specs=[
            pl.BlockSpec((sectors, rows, lons), lambda d: (0, d, 0)),
            pl.BlockSpec((sectors, slots, lons, width), lambda d: (0, 0, 0, 0)),
        ],
        out_specs=pl.BlockSpec((1, slots, rows, width), lambda d: (d, 0, 0, 0)),
        out_shape=jax.ShapeDtypeStruct((bands, slots, rows, width), jnp.bfloat16),
        compiler_params=pltpu.CompilerParams(vmem_limit_bytes=VMEM_BYTES),
        cost_estimate=pl.CostEstimate(
            flops=2 * bands * rows * sectors * lons * slots * width,
            bytes_accessed=2 * (cells.size + table.size + bands * rows * slots * width),
            transcendentals=0,
        ),
    )(table, cells)


def disco_kernel(
    coef_ref, shift_ref, main_ref, prev_ref, next_ref, top_ref, bottom_ref,
    left_ref, right_ref, input_ref, weight_ref, grad_ref, taps_ref, ext_ref, spread_ref,
):
    step, steps = pl.program_id(0), pl.num_programs(0)
    rows, lons, channels = main_ref.shape

    @pl.when(step == 0)
    def _():
        taps_ref[...] = jnp.zeros_like(taps_ref)
        ext_ref[...] = jnp.zeros_like(ext_ref)

    for r in range(rows + 2):
        if r == 0:
            row = jnp.where(step == 0, top_ref[0].astype(jnp.float32), prev_ref[0].astype(jnp.float32))
        elif r == rows + 1:
            row = jnp.where(
                step == steps - 1, bottom_ref[0].astype(jnp.float32), next_ref[0].astype(jnp.float32)
            )
        else:
            row = main_ref[r - 1].astype(jnp.float32)
        ext_ref[r, 8 : 8 + lons] = row
        ext_ref[r, 7:8] = left_ref[step * rows + r]
        ext_ref[r, 8 + lons : 9 + lons] = right_ref[step * rows + r]
    for r in range(rows):
        cycle = step * rows + r
        for k, offset in enumerate((-1, 0, 1)):
            source = r + 1 - offset
            shift = shift_ref[cycle, k]
            picked = jnp.where(
                shift == 0,
                ext_ref[source, 8 : 8 + lons],
                jnp.where(
                    shift == 1, ext_ref[source, 7 : 7 + lons], ext_ref[source, 9 : 9 + lons]
                ),
            )
            spread_ref[:, k * channels : (k + 1) * channels] = (
                coef_ref[cycle, k] * picked
            ).astype(jnp.bfloat16)
        spread = spread_ref[...]
        grad_ref[r] = jnp.dot(spread, weight_ref[...], preferred_element_type=jnp.float32).astype(
            jnp.bfloat16
        )
        taps_ref[...] += lax.dot_general(
            input_ref[r], spread, (((0,), (0,)), ((), ())), preferred_element_type=jnp.float32
        )


def disco(coef, shifts, grad_out, top, bottom, left, right, block_input, weight):
    rows_here, lons, channels = grad_out.shape
    rows = largest_divisor(rows_here, 4)
    steps = rows_here // rows
    wide = weight.shape[0]
    whole = lambda shape: pl.BlockSpec(shape, lambda i: (0,) * len(shape))
    band = pl.BlockSpec((rows, lons, channels), lambda i: (i, 0, 0))
    return pl.pallas_call(
        disco_kernel,
        grid=(steps,),
        in_specs=[
            pl.BlockSpec(memory_space=pltpu.SMEM),
            pl.BlockSpec(memory_space=pltpu.SMEM),
            band,
            pl.BlockSpec((1, lons, channels), lambda i: (jnp.maximum(i * rows - 1, 0), 0, 0)),
            pl.BlockSpec(
                (1, lons, channels), lambda i: (jnp.minimum(i * rows + rows, rows_here - 1), 0, 0)
            ),
            whole(top.shape),
            whole(bottom.shape),
            whole(left.shape),
            whole(right.shape),
            band,
            whole(weight.shape),
        ],
        out_specs=[band, whole((channels, wide))],
        out_shape=[
            jax.ShapeDtypeStruct(grad_out.shape, jnp.bfloat16),
            jax.ShapeDtypeStruct((channels, wide), jnp.float32),
        ],
        scratch_shapes=[
            pltpu.VMEM((rows + 2, (lons + 9 + 15) // 8 * 8, channels), jnp.float32),
            pltpu.VMEM((lons, wide), jnp.bfloat16),
        ],
        compiler_params=pltpu.CompilerParams(vmem_limit_bytes=VMEM_BYTES),
        cost_estimate=pl.CostEstimate(
            flops=8 * rows_here * lons * channels * wide,
            bytes_accessed=6 * grad_out.size,
            transcendentals=0,
        ),
    )(coef, shifts, grad_out, grad_out, grad_out, top, bottom, left, right, block_input, weight)


def neighbours(first, last, axis):
    size = lax.axis_size(axis)
    up = [(i, (i + 1) % size) for i in range(size)]
    down = [(j, i) for i, j in up]
    return lax.ppermute(last, axis, up), lax.ppermute(first, axis, down)


def on_device(
    grad_out, block_input, leg_table, spec_coeff, spec_filter, cycle_weight, cycle_shift, tap_weight
):
    rows_here, lons_here, channels = grad_out.shape
    sectors, bands = lax.axis_size("lon"), lax.axis_size("lat")
    lon_total, cycle_total = lons_here * sectors, rows_here * bands
    orders_here = leg_table.shape[0]
    order_total = orders_here * bands
    lanes = channels // sectors

    top, bottom = neighbours(grad_out[:1], grad_out[-1:], "lat")

    def column(at):
        parts = [block[:, at : at + 1] for block in (top, grad_out, bottom)]
        return jnp.concatenate(parts, axis=0)

    left, right = neighbours(column(0), column(lons_here - 1), "lon")

    packs = largest_divisor(rows_here, max(1, 128 // lanes))
    chunks = largest_divisor(rows_here // packs, 4)
    slots = rows_here // (packs * chunks)
    field = grad_out.reshape(chunks, packs, slots, lons_here, channels)
    table = split_table(sectors, lons_here, order_total)
    packed = [pack(field, k, sectors) for k in range(chunks)]
    packed[0], left, right = lax.optimization_barrier((packed[0], left, right))

    pieces = []
    for k in range(chunks):
        cells = lax.all_to_all(packed[k], "lon", split_axis=0, concat_axis=0, tiled=True)
        part = analyse(table, cells, bands)
        part = lax.all_to_all(part, "lat", split_axis=0, concat_axis=0, tiled=True)
        part = part.reshape(bands, slots, orders_here, 2, packs, lanes)
        part = part.transpose(2, 0, 4, 1, 3, 5)
        pieces.append(part.reshape(orders_here, bands, packs * slots, 2 * lanes))

    cycle_start = lax.axis_index("lat") * rows_here
    weight_pad = jnp.pad(cycle_weight, ((1, 1), (0, 0)))
    shift_pad = jnp.pad(cycle_shift, ((1, 1), (0, 0)))

    def per_tap(padded):
        parts = [
            lax.dynamic_slice_in_dim(padded, cycle_start + 1 - offset, rows_here, 0)[:, k]
            for k, offset in enumerate((-1, 0, 1))
        ]
        return jnp.stack(parts, axis=-1)

    weight = tap_weight.transpose(0, 2, 1).reshape(-1, channels)
    input_grad, taps_part = disco(
        per_tap(weight_pad),
        per_tap(shift_pad),
        grad_out,
        top,
        bottom,
        left.astype(jnp.float32),
        right.astype(jnp.float32),
        block_input,
        weight,
    )
    taps_part = taps_part.reshape(channels, -1, channels).transpose(1, 0, 2)
    taps_grad = lax.psum(taps_part, ("lat", "lon")) / math.sqrt(cycle_total * lon_total)

    by_order = jnp.stack(pieces, axis=2).reshape(orders_here, cycle_total, 2 * lanes)
    degree = jnp.einsum("mla,man->lmn", leg_table, by_order, preferred_element_type=jnp.float32)
    degree = degree.reshape(-1, orders_here, 2, lanes)
    spec_grad = (degree * spec_filter[:, None, None, :]).astype(jnp.bfloat16)
    filter_part = jnp.sum(spec_coeff.astype(jnp.float32) * degree, axis=(1, 2)) / math.sqrt(
        2 * order_total
    )
    filter_grad = lax.psum(filter_part, "lat")
    return (spec_grad, filter_grad, input_grad, taps_grad)


def solution(mesh):
    in_specs = (
        P("lat", "lon", None),
        P("lat", "lon", None),
        P("lat", None, None),
        P(None, "lat", None, "lon"),
        P(None, "lon"),
        P(),
        P(),
        P(),
    )
    out_specs = (P(None, "lat", None, "lon"), P(None, "lon"), P("lat", "lon", None), P())
    return jax.shard_map(
        on_device, mesh=mesh, in_specs=in_specs, out_specs=out_specs, check_vma=False
    )
```

time: 1150 us -> 905 us (0.79)
  local copies, waits for them, and re-layouts: 332 us -> 193 us
  matrix products: 157 us -> 27.7 us
  Pallas kernels: 0 us -> 128 us
  other arithmetic: 118 us -> 46.2 us
  waiting for transfers between devices: 481 us -> 428 us
  starting transfers between devices: 17.1 us -> 49.1 us
    ppermute x4, waiting for transfers between devices: 481 us -> 76.4 us  [neighbours(): return (lax.ppermute(last, axis, up), lax.ppermute(first, axis, down))]
    all_to_all x2 -> x8, waiting for transfers between devices: 0.01 us -> 239 us  [the longest x4 207 us: on_device(): lax.all_to_all(packed[k], 'lon', split_axis=0, concat_axis=0, tiled=True)]
    dot_general x8 -> x1, matrix products: 157 us -> 27.7 us  [on_device(): jnp.einsum('mla,man->lmn', leg_table, by_order, preferred_element_type=jn...]
    pallas_call x0 -> x9, Pallas kernels: none -> 128 us  [the longest x1 59.4 us: disco(): pl.pallas_call(disco_kernel, grid=(steps,), in_specs=[pl.BlockSpec(memory...]
    psum x1, waiting for transfers between devices: 0.01 us -> 112 us  [on_device(): lax.psum(taps_part, ('lat', 'lon')) / math.sqrt(cycle_total * lon_total)]
    all_to_all x4 -> x0, local copies, waits for them, and re-layouts: 112 us -> none  [the longest x2 78.9 us: on_device(): lax.all_to_all(grad_out, 'lon', split_axis=2, concat_axis=1, tiled=True)]
    convert_element_type x5 -> x0, local copies, waits for them, and re-layouts: 90.2 us -> none  [the longest x3 50.9 us: on_device(): (coef[:, None, None] * picked).astype(jnp.bfloat16).reshape(-1, channels)]
    transpose x0 -> x5, local copies, waits for them, and re-layouts: none -> 50.8 us  [the longest x4 50.6 us: on_device(): part = part.transpose(2, 0, 4, 1, 3, 5)]
  transfers between devices with their start and end apart: 7 -> 13, of which waited for: 1 -> 9; matrix products, arithmetic and copies ran while one was open for 45% -> 16% of each run, Pallas kernels for 0% -> 13%
where the time goes in v1:
time: 905 us; the launch traced here: 898 us
  waiting for transfers between devices  428 us (47%)
  local copies, waits for them, and re-layouts  193 us (21%)
  Pallas kernels  128 us (14%)
  starting transfers between devices  49.1 us (5%)
  other arithmetic  46.2 us (5%)
  matrix products  27.7 us (3%)
  between operations  14.3 us (2%)
  blocking collectives  11.5 us (1%)
    all_to_all x4, waiting for transfers between devices, on_device(): lax.all_to_all(packed[k], 'lon', split_axis=0, concat_axis=0, tiled=True)  207 us
    psum x1, waiting for transfers between devices, on_device(): lax.psum(taps_part, ('lat', 'lon')) / math.sqrt(cycle_total * lon_total)  112 us
    ppermute x4, waiting for transfers between devices, neighbours(): return (lax.ppermute(last, axis, up), lax.ppermute(first, axis, down))  76.4 us
    unnamed x28, local copies, waits for them, and re-layouts  73.5 us
    pallas_call x1, Pallas kernels, disco(): pl.pallas_call(disco_kernel, grid=(steps,), in_specs=[pl.BlockSpec(memory...  59.4 us
    transpose x4, local copies, waits for them, and re-layouts, on_device(): part = part.transpose(2, 0, 4, 1, 3, 5)  50.6 us
    reshape x4, local copies, waits for them, and re-layouts, on_device(): part = part.reshape(bands, slots, orders_here, 2, packs, lanes)  47.7 us
    pallas_call x4, Pallas kernels, analyse(): pl.pallas_call(analyse_kernel, grid=(bands,), in_specs=[pl.BlockSpec((sec...  34.7 us
  transfers between devices with their start and end apart: 13, of which 9 were waited for; matrix products, arithmetic and copies ran while one was open for 16% of the time, Pallas kernels for 13%

profile of v1, /device:TPU:12, one launch (start us, length us, event | category | flops | bytes accessed | tf_op | source)
XLA Modules:
  0.0 897.7 jit_solution(9947967112082782726)
XLA Ops:
  7.2 19.0 %copy.46.main_ref.prev_ref.next_ref = bf16[176,180,256]{2,1,0:T(8,128)(2,1)} copy(bf16[176,180,256]{2,0,1:T(8,128)(2,1)} %param.8) | data formatting | bytes 32440320 | tf_op args[0]
  26.1 8.4 shard_map.113
  42.8 8.4 shard_map.115
  53.2 78.4 %all-to-all-done.2.x_ref = bf16[8,11,180,128]{3,2,1,0:T(8,128)(2,1)} async-done(((bf16[8,11,180,128]{3,2,1,0:T(8,128)(2,1)}), bf16[8,11,180,128]{3,2,1,0:T(8,128)(2,1)}, u32[]{:S(2)}, u32[]{:S(2)}) %all-to-all-start.2) | async-done | bytes 4055072 | tf_op jit(solution)/shard_map/all_to_all | solution.py:211
  139.5 8.4 shard_map.117
  149.9 77.8 %all-to-all-done.4.x_ref = bf16[8,11,180,128]{3,2,1,0:T(8,128)(2,1)} async-done(((bf16[8,11,180,128]{3,2,1,0:T(8,128)(2,1)}), bf16[8,11,180,128]{3,2,1,0:T(8,128)(2,1)}, u32[]{:S(2)}, u32[]{:S(2)}) %all-to-all-start.4) | async-done | bytes 4055072 | tf_op jit(solution)/shard_map/all_to_all | solution.py:211
  243.2 8.4 shard_map.111
  253.7 73.9 %collective-permute-done.2 = bf16[178,1,256]{2,1,0:T(2,128)(2,1)S(1)} collective-permute-done((bf16[178,1,256]{2,1,0:T(2,128)(2,1)S(1)}, bf16[178,1,256]{2,1,0:T(2,128)(2,1)S(1)}, u32[]{:S(2)}, u32[]{:S(2)}) %collective-permute-start.2) | collective-permute-done | bytes 91168 | tf_op jit(solution)/shard_map/ppermute | solution.py:180
  334.6 27.8 %multiply_convert_fusion.1.table_ref = bf16[8,768,180]{2,1,0:T(8,128)(2,1)S(1)} fusion(s32[768]{0:T(1024)S(1)} %get-tuple-element.42, s32[768]{0:T(1024)S(1)} %get-tuple-element.45, s32[8]{0:T(128)S(1)} %iota_multiply_fusion, s32[768]{0:T(1024)S(1)} %get-tuple-element.43, s32[768]{0:T(1024)S(1)} %get-tuple-element.44, ...), kind=kLoop, calls=%fused_computation.6 | loop fusion | flops 17694720 | bytes 2225696 | tf_op jit(solution)/shard_map/convert_element_type | solution.py:27
  362.4 8.7 shard_map.114
  372.8 50.8 %all-to-all-done.x_ref = bf16[8,11,180,128]{3,2,1,0:T(8,128)(2,1)} async-done(((bf16[8,11,180,128]{3,2,1,0:T(8,128)(2,1)}), bf16[8,11,180,128]{3,2,1,0:T(8,128)(2,1)}, u32[]{:S(2)}, u32[]{:S(2)}) %all-to-all-start) | async-done | bytes 4055072 | tf_op jit(solution)/shard_map/all_to_all | solution.py:211
  430.0 8.6 shard_map.116
  438.6 15.9 %all-to-all-done.3 = bf16[4,11,192,128]{3,2,1,0:T(8,128)(2,1)} async-done(((bf16[4,11,192,128]{3,2,1,0:T(8,128)(2,1)}), bf16[4,11,192,128]{3,2,1,0:T(8,128)(2,1)}, u32[]{:S(2)}, u32[]{:S(2)}) %all-to-all-start.3) | async-done | bytes 2162720 | tf_op jit(solution)/shard_map/all_to_all | solution.py:213
  460.9 8.7 shard_map.118
  469.6 15.9 %all-to-all-done.5 = bf16[4,11,192,128]{3,2,1,0:T(8,128)(2,1)} async-done(((bf16[4,11,192,128]{3,2,1,0:T(8,128)(2,1)}), bf16[4,11,192,128]{3,2,1,0:T(8,128)(2,1)}, u32[]{:S(2)}, u32[]{:S(2)}) %all-to-all-start.5) | async-done | bytes 2162720 | tf_op jit(solution)/shard_map/all_to_all | solution.py:213
  490.7 19.0 %copy.62.input_ref = bf16[176,180,256]{2,1,0:T(8,128)(2,1)} copy(bf16[176,180,256]{2,0,1:T(8,128)(2,1)} %param.9) | data formatting | bytes 32440320 | tf_op args[1]
  512.2 8.7 shard_map.112
  525.4 59.4 %shard_map.119 = (bf16[176,180,256]{2,1,0:T(8,128)(2,1)}, f32[256,768]{1,0:T(8,128)S(1)}) custom-call(f32[176,3]{1,0:T(8,128)S(1)} %copy.57.coef_ref, s32[176,3]{1,0:T(8,128)S(1)} %copy.58.shift_ref, bf16[176,180,256]{2,1,0:T(8,128)(2,1)} %copy.46.main_ref.prev_ref.next_ref, bf16[176,180,256]{2,1,0:T(8,128)(2,1)} %copy.46.main_ref.prev_ref.next_ref, ...), custom_call_target="tpu_custom_call" | custom-call | flops 49828331520 | bytes 48660480 | tf_op jit(solution)/shard_map/pallas_call | solution.py:140
  586.0 19.1 %copy.64 = bf16[176,180,256]{2,0,1:T(8,128)(2,1)} copy(bf16[176,180,256]{2,1,0:T(8,128)(2,1)} %get-tuple-element.24) | data formatting | bytes 32440320
  605.1 112.3 %all-reduce.4.cloned.1.call-done = f32[3,256,256]{1,2,0:T(8,128)} async-done(((f32[3,256,256]{1,2,0:T(8,128)}), f32[3,256,256]{1,2,0:T(8,128)}) %all-reduce.4.cloned.1.call-update) | async-done | bytes 786448 | tf_op jit(solution)/shard_map/psum | solution.py:242
  719.8 11.9 %reshape.38 = bf16[4,11,96,2,4,32]{5,4,3,2,1,0:T(4,128)(2,1)} reshape(bf16[4,11,192,128]{3,2,1,0:T(8,128)(2,1)} %all-to-all-done.3) | data formatting | bytes 4325376 | tf_op jit(solution)/shard_map/reshape | solution.py:214
  731.7 11.9 %copy.52 = bf16[96,4,4,11,2,32]{0,5,4,3,2,1:T(8,128)(2,1)S(1)} copy(bf16[96,4,4,11,2,32]{5,2,4,0,3,1:T(4,128)(2,1)} %bitcast.36) | data formatting | bytes 4325376 | tf_op jit(solution)/shard_map/transpose | solution.py:215
  743.6 11.9 %reshape.39 = bf16[4,11,96,2,4,32]{5,4,3,2,1,0:T(4,128)(2,1)} reshape(bf16[4,11,192,128]{3,2,1,0:T(8,128)(2,1)} %all-to-all-done.5) | data formatting | bytes 4325376 | tf_op jit(solution)/shard_map/reshape | solution.py:214
  755.6 12.9 %copy.53 = bf16[96,4,4,11,2,32]{0,5,4,3,2,1:T(8,128)(2,1)} copy(bf16[96,4,4,11,2,32]{5,2,4,0,3,1:T(4,128)(2,1)} %bitcast.37) | data formatting | bytes 4325376 | tf_op jit(solution)/shard_map/transpose | solution.py:215
  768.5 11.9 %reshape.40 = bf16[4,11,96,2,4,32]{5,4,3,2,1,0:T(4,128)(2,1)} reshape(bf16[4,11,192,128]{3,2,1,0:T(8,128)(2,1)} %all-to-all-done.7) | data formatting | bytes 4325376 | tf_op jit(solution)/shard_map/reshape | solution.py:214
  780.4 12.9 %copy.54 = bf16[96,4,4,11,2,32]{0,5,4,3,2,1:T(8,128)(2,1)} copy(bf16[96,4,4,11,2,32]{5,2,4,0,3,1:T(4,128)(2,1)} %bitcast.38) | data formatting | bytes 4325376 | tf_op jit(solution)/shard_map/transpose | solution.py:215
  793.3 11.9 %reshape.37 = bf16[4,11,96,2,4,32]{5,4,3,2,1,0:T(4,128)(2,1)} reshape(bf16[4,11,192,128]{3,2,1,0:T(8,128)(2,1)} %all-to-all-done.1) | data formatting | bytes 4325376 | tf_op jit(solution)/shard_map/reshape | solution.py:214
  805.2 12.9 %copy.51 = bf16[96,4,4,11,2,32]{0,5,4,3,2,1:T(8,128)(2,1)} copy(bf16[96,4,4,11,2,32]{5,2,4,0,3,1:T(4,128)(2,1)} %bitcast.39) | data formatting | bytes 4325376 | tf_op jit(solution)/shard_map/transpose | solution.py:215
  818.2 9.8 %pad_maximum_fusion = bf16[96,4,4,44,64]{0,4,3,2,1:T(8,128)(2,1)} fusion(bf16[96,4,1,44,64]{0,4,3,2,1:T(8,128)(2,1)} %bitcast.42, bf16[96,4,1,44,64]{0,4,3,2,1:T(8,128)(2,1)} %bitcast.41, bf16[96,4,1,44,64]{0,4,3,2,1:T(8,128)(2,1)S(1)} %bitcast.40, bf16[96,4,1,44,64]{0,4,3,2,1:T(8,128)(2,1)} %bitcast.43), kind=kLoop, calls=%fused_computation | loop fusion | flops 12976128 | bytes 17301504 | tf_op jit(solution)/shard_map/stack | solution.py:244
  828.0 17.3 %copy.55 = bf16[96,704,64]{1,2,0:T(8,128)(2,1)} copy(bf16[96,704,64]{0,2,1:T(8,128)(2,1)} %bitcast.34) | data formatting | bytes 17301504 | tf_op jit(solution)/shard_map/reshape | solution.py:244
  845.3 27.7 %multiply_convert_fusion = (bf16[384,96,2,32]{0,3,2,1:T(8,128)(2,1)}, f32[96,64,384]{2,1,0:T(8,128)}) fusion(f32[384,32]{0,1:T(8,128)S(1)} %copy-done.9, bf16[96,704,64]{1,2,0:T(8,128)(2,1)} %copy.55, bf16[96,384,704]{1,2,0:T(8,128)(2,1)} %param.10), kind=kOutput, calls=%fused_computation.3 | convolution fusion | flops 3326607360 | bytes 74760192 | tf_op jit(solution)/shard_map/mla,man->lmn/dot_general | solution.py:245
  879.4 11.5 %psum.14 = f32[384,32]{0,1:T(8,128)} all-reduce(f32[384,32]{0,1:T(8,128)S(1)} %broadcast_multiply_fusion.1), channel_id=1, replica_groups=mesh['lat'=4,'lon'=8] {'lat'}, use_global_device_ids=true, to_apply=%region_1.2 | all-reduce | flops 12288 | bytes 98304 | tf_op jit(solution)/shard_map/psum | solution.py:251
  (68 shorter events, 81.0 us)
Async XLA Ops:
  34.6 2.0 copy-start.3
  36.5 95.1 %all-to-all-start.2 = ((bf16[8,11,180,128]{3,2,1,0:T(8,128)(2,1)}), bf16[8,11,180,128]{3,2,1,0:T(8,128)(2,1)}, u32[]{:S(2)}, u32[]{:S(2)}) async-start(bf16[8,11,180,128]{3,2,1,0:T(8,128)(2,1)} %copy-done.3), calls=%async_computation.2 | async-start | bytes 8290304 | tf_op jit(solution)/shard_map/all_to_all | solution.py:211
  51.2 2.0 copy-start.2
  131.6 96.1 %all-to-all-start.4 = ((bf16[8,11,180,128]{3,2,1,0:T(8,128)(2,1)}), bf16[8,11,180,128]{3,2,1,0:T(8,128)(2,1)}, u32[]{:S(2)}, u32[]{:S(2)}) async-start(bf16[8,11,180,128]{3,2,1,0:T(8,128)(2,1)} %copy-done.2), calls=%async_computation.4 | async-start | bytes 8290304 | tf_op jit(solution)/shard_map/all_to_all | solution.py:211
  147.9 2.0 copy-start
  227.7 101.8 %all-to-all-start.6 = ((bf16[8,11,180,128]{3,2,1,0:T(8,128)(2,1)}), bf16[8,11,180,128]{3,2,1,0:T(8,128)(2,1)}, u32[]{:S(2)}, u32[]{:S(2)}) async-start(bf16[8,11,180,128]{3,2,1,0:T(8,128)(2,1)} %copy-done), calls=%async_computation.6 | async-start | bytes 8290304 | tf_op jit(solution)/shard_map/all_to_all | solution.py:211
  236.5 4.0 collective-permute-start
  236.5 4.0 collective-permute-start.1
  240.8 86.7 %collective-permute-start.2 = (bf16[178,1,256]{2,1,0:T(2,128)(2,1)S(1)}, bf16[178,1,256]{2,1,0:T(2,128)(2,1)S(1)}, u32[]{:S(2)}, u32[]{:S(2)}) collective-permute-start(bf16[178,1,256]{2,1,0:T(2,128)(2,1)S(1)} %pad_maximum_fusion.1), channel_id=1, source_target_pairs={{0,1},{1,2},{2,3},{3,4},{4,5},{5,6},{6,7},{7,0},{8,9},{9,10},{10,1... | collective-permute-start | bytes 273416 | tf_op jit(solution)/shard_map/ppermute | solution.py:180
  242.6 86.8 %collective-permute-start.3 = (bf16[178,1,256]{2,1,0:T(2,128)(2,1)S(1)}, bf16[178,1,256]{2,1,0:T(2,128)(2,1)S(1)}, u32[]{:S(2)}, u32[]{:S(2)}) collective-permute-start(bf16[178,1,256]{2,1,0:T(2,128)(2,1)S(1)} %pad_maximum_fusion.2), channel_id=1, source_target_pairs={{1,0},{2,1},{3,2},{4,3},{5,4},{6,5},{7,6},{0,7},{9,8},{10,9},{11,1... | collective-permute-start | bytes 273416 | tf_op jit(solution)/shard_map/ppermute | solution.py:180
  251.7 2.0 copy-start.1
  329.5 94.1 %all-to-all-start = ((bf16[8,11,180,128]{3,2,1,0:T(8,128)(2,1)}), bf16[8,11,180,128]{3,2,1,0:T(8,128)(2,1)}, u32[]{:S(2)}, u32[]{:S(2)}) async-start(bf16[8,11,180,128]{3,2,1,0:T(8,128)(2,1)} %copy-done.1), calls=%async_computation | async-start | bytes 8290304 | tf_op jit(solution)/shard_map/all_to_all | solution.py:211
  371.1 1.7 copy-start.4
  423.6 30.9 %all-to-all-start.3 = ((bf16[4,11,192,128]{3,2,1,0:T(8,128)(2,1)}), bf16[4,11,192,128]{3,2,1,0:T(8,128)(2,1)}, u32[]{:S(2)}, u32[]{:S(2)}) async-start(bf16[4,11,192,128]{3,2,1,0:T(8,128)(2,1)} %shard_map.114), calls=%async_computation.3 | async-start | bytes 4325376 | tf_op jit(solution)/shard_map/all_to_all | solution.py:213
  428.1 1.9 copy-start.5
  454.5 30.9 %all-to-all-start.5 = ((bf16[4,11,192,128]{3,2,1,0:T(8,128)(2,1)}), bf16[4,11,192,128]{3,2,1,0:T(8,128)(2,1)}, u32[]{:S(2)}, u32[]{:S(2)}) async-start(bf16[4,11,192,128]{3,2,1,0:T(8,128)(2,1)} %shard_map.116), calls=%async_computation.5 | async-start | bytes 4325376 | tf_op jit(solution)/shard_map/all_to_all | solution.py:213
  459.0 1.9 copy-start.6
  460.9 29.3 %copy-start.10 = (f32[704,3]{0,1:T(4,128)S(1)}, f32[704,3]{0,1:T(4,128)}, u32[]{:S(2)}) copy-start(f32[704,3]{0,1:T(4,128)} %param.13) | copy-start | bytes 25348
  460.9 29.5 %copy-start.11 = (s32[704,3]{0,1:T(4,128)S(1)}, s32[704,3]{0,1:T(4,128)}, u32[]{:S(2)}) copy-start(s32[704,3]{0,1:T(4,128)} %param.14) | copy-start | bytes 25348
  485.5 35.4 %all-to-all-start.7 = ((bf16[4,11,192,128]{3,2,1,0:T(8,128)(2,1)}), bf16[4,11,192,128]{3,2,1,0:T(8,128)(2,1)}, u32[]{:S(2)}, u32[]{:S(2)}) async-start(bf16[4,11,192,128]{3,2,1,0:T(8,128)(2,1)} %shard_map.118), calls=%async_computation.7 | async-start | bytes 4325376 | tf_op jit(solution)/shard_map/all_to_all | solution.py:213
  490.7 19.1 %copy-start.8 = (bf16[3,256,256]{2,1,0:T(8,128)(2,1)S(1)}, bf16[3,256,256]{2,1,0:T(8,128)(2,1)}, u32[]{:S(2)}) copy-start(bf16[3,256,256]{2,1,0:T(8,128)(2,1)} %param.15) | copy-start | bytes 1179652
  510.3 1.9 copy-start.7
  520.9 272.4 %all-to-all-start.1 = ((bf16[4,11,192,128]{3,2,1,0:T(8,128)(2,1)}), bf16[4,11,192,128]{3,2,1,0:T(8,128)(2,1)}, u32[]{:S(2)}, u32[]{:S(2)}) async-start(bf16[4,11,192,128]{3,2,1,0:T(8,128)(2,1)} %shard_map.112), calls=%async_computation.1 | async-start | bytes 4325376 | tf_op jit(solution)/shard_map/all_to_all | solution.py:213
  525.4 192.1 %all-reduce.4.cloned.1.call-start = ((), (), s32[]{:S(2)}) async-start(), calls=%async_computation.8 | async-start | bytes 1572864 | tf_op jit(solution)/shard_map/psum | solution.py:242
  828.0 17.3 %copy-start.9 = (f32[384,32]{0,1:T(8,128)S(1)}, f32[384,32]{0,1:T(8,128)}, u32[]{:S(2)}) copy-start(f32[384,32]{0,1:T(8,128)} %param.12) | copy-start | bytes 147460
Sparse Core Ops, SparseCore 0:
  586.2 131.2 all-reduce.3

commit v2 on v1

--- a/solution.py
+++ b/solution.py
@@ -180,6 +180,22 @@
     return lax.ppermute(last, axis, up), lax.ppermute(first, axis, down)
 
 
+def swap_bands(blocks, axis):
+    size = lax.axis_size(axis)
+    me = lax.axis_index(axis)
+    by_distance = [lax.dynamic_index_in_dim(blocks, me, 0, keepdims=True)]
+    for step in range(1, size):
+        block = lax.dynamic_index_in_dim(blocks, lax.rem(me + step, size), 0, keepdims=True)
+        pairs = [(i, (i + step) % size) for i in range(size)]
+        by_distance.append(lax.ppermute(block, axis, pairs))
+    stacked = jnp.concatenate(by_distance, axis=0)
+    ordered = [
+        lax.dynamic_index_in_dim(stacked, lax.rem(me - b + size, size), 0, keepdims=True)
+        for b in range(size)
+    ]
+    return jnp.concatenate(ordered, axis=0)
+
+
 def on_device(
     grad_out, block_input, leg_table, spec_coeff, spec_filter, cycle_weight, cycle_shift, tap_weight
 ):
@@ -204,16 +220,6 @@
     field = grad_out.reshape(chunks, packs, slots, lons_here, channels)
     table = split_table(sectors, lons_here, order_total)
     packed = [pack(field, k, sectors) for k in range(chunks)]
-    packed[0], left, right = lax.optimization_barrier((packed[0], left, right))
-
-    pieces = []
-    for k in range(chunks):
-        cells = lax.all_to_all(packed[k], "lon", split_axis=0, concat_axis=0, tiled=True)
-        part = analyse(table, cells, bands)
-        part = lax.all_to_all(part, "lat", split_axis=0, concat_axis=0, tiled=True)
-        part = part.reshape(bands, slots, orders_here, 2, packs, lanes)
-        part = part.transpose(2, 0, 4, 1, 3, 5)
-        pieces.append(part.reshape(orders_here, bands, packs * slots, 2 * lanes))
 
     cycle_start = lax.axis_index("lat") * rows_here
     weight_pad = jnp.pad(cycle_weight, ((1, 1), (0, 0)))
@@ -238,8 +244,36 @@
         block_input,
         weight,
     )
-    taps_part = taps_part.reshape(channels, -1, channels).transpose(1, 0, 2)
-    taps_grad = lax.psum(taps_part, ("lat", "lon")) / math.sqrt(cycle_total * lon_total)
+
+    def reduce_taps(part):
+        part = part.reshape(channels, -1, channels).transpose(1, 0, 2)
+        return lax.psum(part, ("lat", "lon")) / math.sqrt(cycle_total * lon_total)
+
+    barrier = lax.optimization_barrier
+    pieces = []
+    previous = None
+    for k in range(chunks):
+        sent = packed[k]
+        if previous is not None:
+            sent, previous = barrier((sent, previous))
+        if k == 2:
+            sent, input_grad, taps_part = barrier((sent, input_grad, taps_part))
+        if k == 3:
+            sent, pieces[0] = barrier((sent, pieces[0]))
+        cells = lax.all_to_all(sent, "lon", split_axis=0, concat_axis=0, tiled=True)
+        previous = cells
+        if k == 2:
+            taps_grad = reduce_taps(taps_part)
+        if k == 3:
+            cells, pieces[1], pieces[2], taps_grad = barrier(
+                (cells, pieces[1], pieces[2], taps_grad)
+            )
+        part = swap_bands(analyse(table, cells, bands), "lat")
+        part = part.reshape(bands, slots, orders_here, 2, packs, lanes)
+        part = part.transpose(2, 0, 4, 1, 3, 5)
+        pieces.append(part.reshape(orders_here, bands, packs * slots, 2 * lanes))
+    if chunks < 3:
+        taps_grad = reduce_taps(taps_part)
 
     by_order = jnp.stack(pieces, axis=2).reshape(orders_here, cycle_total, 2 * lanes)
     degree = jnp.einsum("mla,man->lmn", leg_table, by_order, preferred_element_type=jnp.float32)

time: 905 us -> 809 us (0.89)
  waiting for transfers between devices: 428 us -> 333 us
  local copies, waits for them, and re-layouts: 193 us -> 183 us
    all_to_all x8 -> x4, waiting for transfers between devices: 239 us -> 83.7 us  [on_device(): cells = lax.all_to_all(sent, 'lon', split_axis=0, concat_axis=0, tiled=True)]
    psum x1, waiting for transfers between devices: 112 us -> 179 us  [reduce_taps(): return lax.psum(part, ('lat', 'lon')) / math.sqrt(cycle_total * lon_total)]
    ppermute x4, waiting for transfers between devices: 76.4 us -> 55.9 us  [neighbours(): return (lax.ppermute(last, axis, up), lax.ppermute(first, axis, down))]
    all_to_all x8 -> x4, starting transfers between devices: 45.1 us -> 27.6 us  [on_device(): cells = lax.all_to_all(sent, 'lon', split_axis=0, concat_axis=0, tiled=True)]
    ppermute x0 -> x12, waiting for transfers between devices: none -> 14 us  [swap_bands(): by_distance.append(lax.ppermute(block, axis, pairs))]
    reshape x4, local copies, waits for them, and re-layouts: 47.7 us -> 36.2 us  [on_device(): part = part.reshape(bands, slots, orders_here, 2, packs, lanes)]
    ppermute x0 -> x12, starting transfers between devices: none -> 11.1 us  [swap_bands(): by_distance.append(lax.ppermute(block, axis, pairs))]
    unnamed x28 -> x32, local copies, waits for them, and re-layouts: 73.5 us -> 68 us
  transfers between devices with their start and end apart: 13 -> 21, of which waited for: 9 -> 8; matrix products, arithmetic and copies ran while one was open for 16% -> 19% of each run, Pallas kernels for 13% -> 14%
where the time goes in v2:
time: 809 us; the launch traced here: 796 us
  waiting for transfers between devices  333 us (41%)
  local copies, waits for them, and re-layouts  183 us (23%)
  Pallas kernels  126 us (16%)
  other arithmetic  55 us (7%)
  starting transfers between devices  43.7 us (5%)
  matrix products  27.4 us (3%)
  between operations  14.9 us (2%)
  blocking collectives  13 us (2%)
    psum x1, waiting for transfers between devices, reduce_taps(): return lax.psum(part, ('lat', 'lon')) / math.sqrt(cycle_total * lon_total)  179 us
    all_to_all x4, waiting for transfers between devices, on_device(): cells = lax.all_to_all(sent, 'lon', split_axis=0, concat_axis=0, tiled=True)  83.7 us
    unnamed x32, local copies, waits for them, and re-layouts  68 us
    pallas_call x1, Pallas kernels, disco(): pl.pallas_call(disco_kernel, grid=(steps,), in_specs=[pl.BlockSpec(memory...  59.3 us
    ppermute x4, waiting for transfers between devices, neighbours(): return (lax.ppermute(last, axis, up), lax.ppermute(first, axis, down))  55.9 us
    transpose x4, local copies, waits for them, and re-layouts, on_device(): part = part.transpose(2, 0, 4, 1, 3, 5)  51.7 us
    reshape x4, local copies, waits for them, and re-layouts, on_device(): part = part.reshape(bands, slots, orders_here, 2, packs, lanes)  36.2 us
    pallas_call x4, Pallas kernels, pack(): pl.pallas_call(functools.partial(pack_kernel, groups, lanes), grid=(slots...  33.7 us
  transfers between devices with their start and end apart: 21, of which 8 were waited for; matrix products, arithmetic and copies ran while one was open for 19% of the time, Pallas kernels for 14%

profile of v2, /device:TPU:12, one launch (start us, length us, event | category | flops | bytes accessed | tf_op | source)
XLA Modules:
  0.0 795.9 jit_solution(6968863083246879443)
XLA Ops:
  7.2 19.0 %copy.46.main_ref.prev_ref.next_ref = bf16[176,180,256]{2,1,0:T(8,128)(2,1)} copy(bf16[176,180,256]{2,0,1:T(8,128)(2,1)} %param.8) | data formatting | bytes 32440320 | tf_op args[0]
  26.2 8.4 %shard_map.114 = bf16[8,11,180,128]{3,2,1,0:T(8,128)(2,1)S(1)} custom-call(bf16[4,4,11,180,256]{4,3,2,1,0:T(8,128)(2,1)} %bitcast.33), custom_call_target="tpu_custom_call" | custom-call | bytes 8110080 | tf_op jit(solution)/shard_map/pallas_call | solution.py:40
  36.6 6.2 all-to-all-start
  42.8 8.4 %shard_map.113 = bf16[8,11,180,128]{3,2,1,0:T(8,128)(2,1)S(1)} custom-call(bf16[4,4,11,180,256]{4,3,2,1,0:T(8,128)(2,1)} %bitcast.34), custom_call_target="tpu_custom_call" | custom-call | bytes 8110080 | tf_op jit(solution)/shard_map/pallas_call | solution.py:40
  53.3 78.4 %all-to-all-done.x_ref = bf16[8,11,180,128]{3,2,1,0:T(8,128)(2,1)} async-done(((bf16[8,11,180,128]{3,2,1,0:T(8,128)(2,1)}), bf16[8,11,180,128]{3,2,1,0:T(8,128)(2,1)}, u32[]{:S(2)}, u32[]{:S(2)}) %all-to-all-start) | async-done | bytes 4055072 | tf_op jit(solution)/shard_map/all_to_all | solution.py:263
  131.7 7.8 all-to-all-start.1
  142.2 8.5 %shard_map.112 = bf16[8,11,180,128]{3,2,1,0:T(8,128)(2,1)S(1)} custom-call(bf16[4,4,11,180,256]{4,3,2,1,0:T(8,128)(2,1)} %bitcast.35), custom_call_target="tpu_custom_call" | custom-call | bytes 8110080 | tf_op jit(solution)/shard_map/pallas_call | solution.py:40
  158.4 19.0 %copy.57.input_ref = bf16[176,180,256]{2,1,0:T(8,128)(2,1)} copy(bf16[176,180,256]{2,0,1:T(8,128)(2,1)} %param.9) | data formatting | bytes 32440320 | tf_op args[1]
  177.6 55.9 %collective-permute-done.3 = bf16[178,1,256]{2,1,0:T(2,128)(2,1)S(1)} collective-permute-done((bf16[178,1,256]{2,1,0:T(2,128)(2,1)S(1)}, bf16[178,1,256]{2,1,0:T(2,128)(2,1)S(1)}, u32[]{:S(2)}, u32[]{:S(2)}) %collective-permute-start.3) | collective-permute-done | bytes 91168 | tf_op jit(solution)/shard_map/ppermute | solution.py:180
  233.9 59.3 %shard_map.115 = (bf16[176,180,256]{2,1,0:T(8,128)(2,1)}, f32[256,768]{1,0:T(8,128)S(1)}) custom-call(f32[176,3]{1,0:T(8,128)S(1)} %copy.52.coef_ref, s32[176,3]{1,0:T(8,128)S(1)} %copy.53.shift_ref, bf16[176,180,256]{2,1,0:T(8,128)(2,1)} %copy.46.main_ref.prev_ref.next_ref, bf16[176,180,256]{2,1,0:T(8,128)(2,1)} %copy.46.main_ref.prev_ref.next_ref, ...), custom_call_target="tpu_custom_call" | custom-call | flops 49828331520 | bytes 48660480 | tf_op jit(solution)/shard_map/pallas_call | solution.py:140
  298.0 27.8 %multiply_convert_fusion.1.table_ref = bf16[8,768,180]{2,1,0:T(8,128)(2,1)S(1)} fusion(s32[768]{0:T(1024)S(1)} %get-tuple-element.94, s32[768]{0:T(1024)S(1)} %get-tuple-element.97, s32[8]{0:T(128)S(1)} %iota_multiply_fusion, s32[768]{0:T(1024)S(1)} %get-tuple-element.95, s32[768]{0:T(1024)S(1)} %get-tuple-element.96, ...), kind=kLoop, calls=%fused_computation.6 | loop fusion | flops 17694720 | bytes 2225696 | tf_op jit(solution)/shard_map/convert_element_type | solution.py:27
  325.8 8.9 %shard_map.116 = bf16[4,11,192,128]{3,2,1,0:T(8,128)(2,1)S(1)} custom-call(bf16[8,768,180]{2,1,0:T(8,128)(2,1)S(1)} %multiply_convert_fusion.1.table_ref, bf16[8,11,180,128]{3,2,1,0:T(8,128)(2,1)} %all-to-all-done.x_ref), custom_call_target="tpu_custom_call" | custom-call | flops 3114270720 | bytes 8429568 | tf_op jit(solution)/shard_map/pallas_call | solution.py:67
  338.9 8.4 %shard_map.111 = bf16[8,11,180,128]{3,2,1,0:T(8,128)(2,1)S(1)} custom-call(bf16[4,4,11,180,256]{4,3,2,1,0:T(8,128)(2,1)} %bitcast.36), custom_call_target="tpu_custom_call" | custom-call | bytes 8110080 | tf_op jit(solution)/shard_map/pallas_call | solution.py:40
  351.3 10.0 %collective-permute-done.6 = bf16[1,11,192,128]{3,2,1,0:T(8,128)(2,1)S(1)} collective-permute-done((bf16[1,11,192,128]{3,2,1,0:T(8,128)(2,1)S(1)}, bf16[1,11,192,128]{3,2,1,0:T(8,128)(2,1)S(1)}, u32[]{:S(2)}, u32[]{:S(2)}) %collective-permute-start.6) | collective-permute-done | bytes 540704 | tf_op jit(solution)/shard_map/ppermute | solution.py:190
  368.2 12.9 %copy.58 = bf16[96,4,4,11,2,32]{0,5,4,3,2,1:T(8,128)(2,1)} copy(bf16[96,4,4,11,2,32]{5,2,4,0,3,1:T(4,128)(2,1)} %bitcast.39) | data formatting | bytes 4325376 | tf_op jit(solution)/shard_map/transpose | solution.py:273
  386.4 8.9 %all-to-all-start.3 = ((bf16[8,11,180,128]{3,2,1,0:T(8,128)(2,1)}), bf16[8,11,180,128]{3,2,1,0:T(8,128)(2,1)}, u32[]{:S(2)}, u32[]{:S(2)}) async-start(bf16[8,11,180,128]{3,2,1,0:T(8,128)(2,1)} %copy-done.1), calls=%async_computation.3 | async-start | bytes 8290304 | tf_op jit(solution)/shard_map/all_to_all | solution.py:263
  398.5 7.9 shard_map.117
  410.8 179.4 %all-reduce.4.cloned.1.call-done = f32[3,256,256]{1,2,0:T(8,128)} async-done(((f32[3,256,256]{1,2,0:T(8,128)}), f32[3,256,256]{1,2,0:T(8,128)}) %all-reduce.4.cloned.1.call-update) | async-done | bytes 786448 | tf_op jit(solution)/shard_map/psum | solution.py:250
  592.2 7.9 shard_map.118
  607.2 11.8 %reshape.49 = bf16[4,11,96,2,4,32]{5,4,3,2,1,0:T(4,128)(2,1)} reshape(bf16[4,11,192,128]{3,2,1,0:T(8,128)(2,1)} %pad_maximum_fusion.4) | data formatting | bytes 4325376 | tf_op jit(solution)/shard_map/reshape | solution.py:272
  619.0 12.9 %copy.59 = bf16[96,4,4,11,2,32]{0,5,4,3,2,1:T(8,128)(2,1)} copy(bf16[96,4,4,11,2,32]{5,2,4,0,3,1:T(4,128)(2,1)} %bitcast.40) | data formatting | bytes 4325376 | tf_op jit(solution)/shard_map/transpose | solution.py:273
  635.6 11.8 %reshape.51 = bf16[4,11,96,2,4,32]{5,4,3,2,1,0:T(4,128)(2,1)} reshape(bf16[4,11,192,128]{3,2,1,0:T(8,128)(2,1)} %pad_maximum_fusion.6) | data formatting | bytes 4325376 | tf_op jit(solution)/shard_map/reshape | solution.py:272
  647.4 12.9 %copy.60 = bf16[96,4,4,11,2,32]{0,5,4,3,2,1:T(8,128)(2,1)} copy(bf16[96,4,4,11,2,32]{5,2,4,0,3,1:T(4,128)(2,1)} %bitcast.41) | data formatting | bytes 4325376 | tf_op jit(solution)/shard_map/transpose | solution.py:273
  660.3 7.9 shard_map.119
  672.4 19.0 %copy.64 = bf16[176,180,256]{2,0,1:T(8,128)(2,1)} copy(bf16[176,180,256]{2,1,0:T(8,128)(2,1)} %get-tuple-element.42) | data formatting | bytes 32440320
  695.3 6.3 reshape.54
  701.6 13.0 %copy.62 = bf16[96,4,4,11,2,32]{0,5,4,3,2,1:T(8,128)(2,1)} copy(bf16[96,4,4,11,2,32]{5,2,4,0,3,1:T(4,128)(2,1)} %bitcast.42) | data formatting | bytes 4325376 | tf_op jit(solution)/shard_map/transpose | solution.py:273
  714.7 9.8 %pad_maximum_fusion = bf16[96,4,4,44,64]{0,4,3,2,1:T(8,128)(2,1)} fusion(bf16[96,4,1,44,64]{0,4,3,2,1:T(8,128)(2,1)} %bitcast.46, bf16[96,4,1,44,64]{0,4,3,2,1:T(8,128)(2,1)} %bitcast.45, bf16[96,4,1,44,64]{0,4,3,2,1:T(8,128)(2,1)} %bitcast.44, bf16[96,4,1,44,64]{0,4,3,2,1:T(8,128)(2,1)S(1)} %bitcast.43), kind=kLoop, calls=%fused_computation | loop fusion | flops 12976128 | bytes 17301504 | tf_op jit(solution)/shard_map/stack | solution.py:278
  724.5 17.2 %copy.63 = bf16[96,704,64]{1,2,0:T(8,128)(2,1)} copy(bf16[96,704,64]{0,2,1:T(8,128)(2,1)} %bitcast.37) | data formatting | bytes 17301504 | tf_op jit(solution)/shard_map/reshape | solution.py:278
  741.7 27.4 %multiply_convert_fusion = (bf16[384,96,2,32]{0,3,2,1:T(8,128)(2,1)}, f32[96,64,384]{2,1,0:T(8,128)}) fusion(f32[384,32]{0,1:T(8,128)S(1)} %copy-done.11, bf16[96,704,64]{1,2,0:T(8,128)(2,1)} %copy.63, bf16[96,384,704]{1,2,0:T(8,128)(2,1)} %param.10), kind=kOutput, calls=%fused_computation.3 | convolution fusion | flops 3326607360 | bytes 74760192 | tf_op jit(solution)/shard_map/mla,man->lmn/dot_general | solution.py:279
  769.2 6.4 multiply_reduce_fusion
  775.6 13.0 %psum.15 = f32[384,32]{0,1:T(8,128)} all-reduce(f32[384,32]{0,1:T(8,128)S(1)} %broadcast_multiply_fusion.1), channel_id=1, replica_groups=mesh['lat'=4,'lon'=8] {'lat'}, use_global_device_ids=true, to_apply=%region_2.3 | all-reduce | flops 12288 | bytes 98304 | tf_op jit(solution)/shard_map/psum | solution.py:285
  (104 shorter events, 68.3 us)
Async XLA Ops:
  34.6 2.0 copy-start.3
  36.6 95.1 %all-to-all-start = ((bf16[8,11,180,128]{3,2,1,0:T(8,128)(2,1)}), bf16[8,11,180,128]{3,2,1,0:T(8,128)(2,1)}, u32[]{:S(2)}, u32[]{:S(2)}) async-start(bf16[8,11,180,128]{3,2,1,0:T(8,128)(2,1)} %copy-done.3), calls=%async_computation | async-start | bytes 8290304 | tf_op jit(solution)/shard_map/all_to_all | solution.py:263
  51.3 2.0 copy-start.2
  131.7 161.5 %all-to-all-start.1 = ((bf16[8,11,180,128]{3,2,1,0:T(8,128)(2,1)}), bf16[8,11,180,128]{3,2,1,0:T(8,128)(2,1)}, u32[]{:S(2)}, u32[]{:S(2)}) async-start(bf16[8,11,180,128]{3,2,1,0:T(8,128)(2,1)} %copy-done.2), calls=%async_computation.1 | async-start | bytes 8290304 | tf_op jit(solution)/shard_map/all_to_all | solution.py:263
  140.4 14.2 %collective-permute-start = (bf16[1,180,256]{2,1,0:T(8,128)(2,1)S(1)}, bf16[1,180,256]{2,1,0:T(8,128)(2,1)S(1)}, u32[]{:S(2)}, u32[]{:S(2)}) collective-permute-start(bf16[1,180,256]{2,1,0:T(8,128)(2,1)S(1)} %get-tuple-element.47), channel_id=1, source_target_pairs={{0,8},{8,16},{16,24},{24,0},{1,9},{9,17},{17,25},{25,1},{2,10},{10... | collective-permute-start | bytes 276488 | tf_op jit(solution)/shard_map/ppermute | solution.py:180
  140.5 14.2 %collective-permute-start.1 = (bf16[1,180,256]{2,1,0:T(8,128)(2,1)S(1)}, bf16[1,180,256]{2,1,0:T(8,128)(2,1)S(1)}, u32[]{:S(2)}, u32[]{:S(2)}) collective-permute-start(bf16[1,180,256]{2,1,0:T(8,128)(2,1)S(1)} %get-tuple-element.46), channel_id=1, source_target_pairs={{8,0},{16,8},{24,16},{0,24},{9,1},{17,9},{25,17},{1,25},{10,2},{18... | collective-permute-start | bytes 276488 | tf_op jit(solution)/shard_map/ppermute | solution.py:180
  142.2 10.4 %copy-start.12 = (f32[704,3]{0,1:T(4,128)S(1)}, f32[704,3]{0,1:T(4,128)}, u32[]{:S(2)}) copy-start(f32[704,3]{0,1:T(4,128)} %param.13) | copy-start | bytes 25348
  142.2 12.3 %copy-start.13 = (s32[704,3]{0,1:T(4,128)S(1)}, s32[704,3]{0,1:T(4,128)}, u32[]{:S(2)}) copy-start(s32[704,3]{0,1:T(4,128)} %param.14) | copy-start | bytes 25348
  155.0 78.5 %collective-permute-start.3 = (bf16[178,1,256]{2,1,0:T(2,128)(2,1)S(1)}, bf16[178,1,256]{2,1,0:T(2,128)(2,1)S(1)}, u32[]{:S(2)}, u32[]{:S(2)}) collective-permute-start(bf16[178,1,256]{2,1,0:T(2,128)(2,1)S(1)} %pad_maximum_fusion.10), channel_id=1, source_target_pairs={{1,0},{2,1},{3,2},{4,3},{5,4},{6,5},{7,6},{0,7},{9,8},{10,9},{11,1... | collective-permute-start | bytes 273416 | tf_op jit(solution)/shard_map/ppermute | solution.py:180
  155.9 77.8 %collective-permute-start.2 = (bf16[178,1,256]{2,1,0:T(2,128)(2,1)S(1)}, bf16[178,1,256]{2,1,0:T(2,128)(2,1)S(1)}, u32[]{:S(2)}, u32[]{:S(2)}) collective-permute-start(bf16[178,1,256]{2,1,0:T(2,128)(2,1)S(1)} %pad_maximum_fusion.9), channel_id=1, source_target_pairs={{0,1},{1,2},{2,3},{3,4},{4,5},{5,6},{6,7},{7,0},{8,9},{9,10},{10,1... | collective-permute-start | bytes 273416 | tf_op jit(solution)/shard_map/ppermute | solution.py:180
  158.4 19.0 %copy-start.10 = (bf16[3,256,256]{2,1,0:T(8,128)(2,1)S(1)}, bf16[3,256,256]{2,1,0:T(8,128)(2,1)}, u32[]{:S(2)}) copy-start(bf16[3,256,256]{2,1,0:T(8,128)(2,1)} %param.15) | copy-start | bytes 1179652
  293.2 93.2 %all-to-all-start.2 = ((bf16[8,11,180,128]{3,2,1,0:T(8,128)(2,1)}), bf16[8,11,180,128]{3,2,1,0:T(8,128)(2,1)}, u32[]{:S(2)}, u32[]{:S(2)}) async-start(bf16[8,11,180,128]{3,2,1,0:T(8,128)(2,1)} %copy-done), calls=%async_computation.2 | async-start | bytes 8290304 | tf_op jit(solution)/shard_map/all_to_all | solution.py:263
  325.8 9.0 %copy-start.4 = (bf16[8,768,180]{2,1,0:T(8,128)(2,1)}, bf16[8,768,180]{2,1,0:T(8,128)(2,1)S(1)}, u32[]{:S(2)}) copy-start(bf16[8,768,180]{2,1,0:T(8,128)(2,1)S(1)} %multiply_convert_fusion.1.table_ref) | copy-start | bytes 6635524
  335.9 14.2 %collective-permute-start.4 = (bf16[1,11,192,128]{3,2,1,0:T(8,128)(2,1)}, bf16[1,11,192,128]{3,2,1,0:T(8,128)(2,1)S(1)}, u32[]{:S(2)}, u32[]{:S(2)}) collective-permute-start(bf16[1,11,192,128]{3,2,1,0:T(8,128)(2,1)} %get-tuple-element.79), channel_id=1, source_target_pairs={{0,8},{8,16},{16,24},{24,0},{1,9},{9,17},{17,25},{25,1},{2,10},{10... | collective-permute-start | bytes 1622024 | tf_op jit(solution)/shard_map/ppermute | solution.py:190
  335.9 15.3 %collective-permute-start.5 = (bf16[1,11,192,128]{3,2,1,0:T(8,128)(2,1)}, bf16[1,11,192,128]{3,2,1,0:T(8,128)(2,1)S(1)}, u32[]{:S(2)}, u32[]{:S(2)}) collective-permute-start(bf16[1,11,192,128]{3,2,1,0:T(8,128)(2,1)} %get-tuple-element.78), channel_id=1, source_target_pairs={{0,16},{8,24},{16,0},{24,8},{1,17},{9,25},{17,1},{25,9},{2,18},{10... | collective-permute-start | bytes 1622024 | tf_op jit(solution)/shard_map/ppermute | solution.py:190
  337.4 23.9 %collective-permute-start.6 = (bf16[1,11,192,128]{3,2,1,0:T(8,128)(2,1)S(1)}, bf16[1,11,192,128]{3,2,1,0:T(8,128)(2,1)S(1)}, u32[]{:S(2)}, u32[]{:S(2)}) collective-permute-start(bf16[1,11,192,128]{3,2,1,0:T(8,128)(2,1)S(1)} %get-tuple-element.77), channel_id=1, source_target_pairs={{0,24},{8,0},{16,8},{24,16},{1,25},{9,1},{17,9},{25,17},{2,26},{10... | collective-permute-start | bytes 1622024 | tf_op jit(solution)/shard_map/ppermute | solution.py:190
  386.4 273.9 %all-to-all-start.3 = ((bf16[8,11,180,128]{3,2,1,0:T(8,128)(2,1)}), bf16[8,11,180,128]{3,2,1,0:T(8,128)(2,1)}, u32[]{:S(2)}, u32[]{:S(2)}) async-start(bf16[8,11,180,128]{3,2,1,0:T(8,128)(2,1)} %copy-done.1), calls=%async_computation.3 | async-start | bytes 8290304 | tf_op jit(solution)/shard_map/all_to_all | solution.py:263
  395.3 194.9 %all-reduce.4.cloned.1.call-start = ((), (), s32[]{:S(2)}) async-start(), calls=%async_computation.4 | async-start | bytes 1572864 | tf_op jit(solution)/shard_map/psum | solution.py:250
  406.4 185.8 %copy-start.6 = (bf16[8,768,180]{2,1,0:T(8,128)(2,1)S(1)}, bf16[8,768,180]{2,1,0:T(8,128)(2,1)}, u32[]{:S(2)}) copy-start(bf16[8,768,180]{2,1,0:T(8,128)(2,1)} %copy-done.4) | copy-start | bytes 6635524
  407.8 194.4 %collective-permute-start.7 = (bf16[1,11,192,128]{3,2,1,0:T(8,128)(2,1)}, bf16[1,11,192,128]{3,2,1,0:T(8,128)(2,1)}, u32[]{:S(2)}, u32[]{:S(2)}) collective-permute-start(bf16[1,11,192,128]{3,2,1,0:T(8,128)(2,1)} %get-tuple-element.71), channel_id=1, source_target_pairs={{0,8},{8,16},{16,24},{24,0},{1,9},{9,17},{17,25},{25,1},{2,10},{10... | collective-permute-start | bytes 1622024 | tf_op jit(solution)/shard_map/ppermute | solution.py:190
  407.8 195.9 %collective-permute-start.8 = (bf16[1,11,192,128]{3,2,1,0:T(8,128)(2,1)}, bf16[1,11,192,128]{3,2,1,0:T(8,128)(2,1)}, u32[]{:S(2)}, u32[]{:S(2)}) collective-permute-start(bf16[1,11,192,128]{3,2,1,0:T(8,128)(2,1)} %get-tuple-element.70), channel_id=1, source_target_pairs={{0,16},{8,24},{16,0},{24,8},{1,17},{9,25},{17,1},{25,9},{2,18},{10... | collective-permute-start | bytes 1622024 | tf_op jit(solution)/shard_map/ppermute | solution.py:190
  409.4 194.3 %collective-permute-start.9 = (bf16[1,11,192,128]{3,2,1,0:T(8,128)(2,1)}, bf16[1,11,192,128]{3,2,1,0:T(8,128)(2,1)}, u32[]{:S(2)}, u32[]{:S(2)}) collective-permute-start(bf16[1,11,192,128]{3,2,1,0:T(8,128)(2,1)} %get-tuple-element.69), channel_id=1, source_target_pairs={{0,24},{8,0},{16,8},{24,16},{1,25},{9,1},{17,9},{25,17},{2,26},{10... | collective-permute-start | bytes 1622024 | tf_op jit(solution)/shard_map/ppermute | solution.py:190
  600.1 3.6 copy-start.9
  601.6 30.4 %collective-permute-start.10 = (bf16[1,11,192,128]{3,2,1,0:T(8,128)(2,1)}, bf16[1,11,192,128]{3,2,1,0:T(8,128)(2,1)}, u32[]{:S(2)}, u32[]{:S(2)}) collective-permute-start(bf16[1,11,192,128]{3,2,1,0:T(8,128)(2,1)} %get-tuple-element.63), channel_id=1, source_target_pairs={{0,8},{8,16},{16,24},{24,0},{1,9},{9,17},{17,25},{25,1},{2,10},{10... | collective-permute-start | bytes 1622024 | tf_op jit(solution)/shard_map/ppermute | solution.py:190
  601.6 30.4 %collective-permute-start.11 = (bf16[1,11,192,128]{3,2,1,0:T(8,128)(2,1)}, bf16[1,11,192,128]{3,2,1,0:T(8,128)(2,1)}, u32[]{:S(2)}, u32[]{:S(2)}) collective-permute-start(bf16[1,11,192,128]{3,2,1,0:T(8,128)(2,1)} %get-tuple-element.62), channel_id=1, source_target_pairs={{0,16},{8,24},{16,0},{24,8},{1,17},{9,25},{17,1},{25,9},{2,18},{10... | collective-permute-start | bytes 1622024 | tf_op jit(solution)/shard_map/ppermute | solution.py:190
  602.3 29.7 %collective-permute-start.12 = (bf16[1,11,192,128]{3,2,1,0:T(8,128)(2,1)}, bf16[1,11,192,128]{3,2,1,0:T(8,128)(2,1)}, u32[]{:S(2)}, u32[]{:S(2)}) collective-permute-start(bf16[1,11,192,128]{3,2,1,0:T(8,128)(2,1)} %get-tuple-element.61), channel_id=1, source_target_pairs={{0,24},{8,0},{16,8},{24,16},{1,25},{9,1},{17,9},{25,17},{2,26},{10... | collective-permute-start | bytes 1622024 | tf_op jit(solution)/shard_map/ppermute | solution.py:190
  669.3 23.3 %collective-permute-start.13 = (bf16[1,11,192,128]{3,2,1,0:T(8,128)(2,1)}, bf16[1,11,192,128]{3,2,1,0:T(8,128)(2,1)S(1)}, u32[]{:S(2)}, u32[]{:S(2)}) collective-permute-start(bf16[1,11,192,128]{3,2,1,0:T(8,128)(2,1)} %get-tuple-element.55), channel_id=1, source_target_pairs={{0,8},{8,16},{16,24},{24,0},{1,9},{9,17},{17,25},{25,1},{2,10},{10... | collective-permute-start | bytes 1622024 | tf_op jit(solution)/shard_map/ppermute | solution.py:190
  669.3 23.3 %collective-permute-start.14 = (bf16[1,11,192,128]{3,2,1,0:T(8,128)(2,1)}, bf16[1,11,192,128]{3,2,1,0:T(8,128)(2,1)S(1)}, u32[]{:S(2)}, u32[]{:S(2)}) collective-permute-start(bf16[1,11,192,128]{3,2,1,0:T(8,128)(2,1)} %get-tuple-element.54), channel_id=1, source_target_pairs={{0,16},{8,24},{16,0},{24,8},{1,17},{9,25},{17,1},{25,9},{2,18},{10... | collective-permute-start | bytes 1622024 | tf_op jit(solution)/shard_map/ppermute | solution.py:190
  670.7 20.7 %copy-start.8 = (f32[3,256,256]{1,2,0:T(8,128)S(1)}, f32[3,256,256]{1,2,0:T(8,128)}, u32[]{:S(2)}) copy-start(f32[3,256,256]{1,2,0:T(8,128)} %broadcast_multiply_fusion) | copy-start | bytes 2359300
  670.8 23.9 %collective-permute-start.15 = (bf16[1,11,192,128]{3,2,1,0:T(8,128)(2,1)S(1)}, bf16[1,11,192,128]{3,2,1,0:T(8,128)(2,1)S(1)}, u32[]{:S(2)}, u32[]{:S(2)}) collective-permute-start(bf16[1,11,192,128]{3,2,1,0:T(8,128)(2,1)S(1)} %get-tuple-element.53), channel_id=1, source_target_pairs={{0,24},{8,0},{16,8},{24,16},{1,25},{9,1},{17,9},{25,17},{2,26},{10... | collective-permute-start | bytes 1622024 | tf_op jit(solution)/shard_map/ppermute | solution.py:190
  701.6 13.0 %copy-start.7 = (bf16[96,4,4,11,2,32]{0,5,4,3,2,1:T(8,128)(2,1)S(1)}, bf16[96,4,4,11,2,32]{0,5,4,3,2,1:T(8,128)(2,1)}, u32[]{:S(2)}) copy-start(bf16[96,4,4,11,2,32]{0,5,4,3,2,1:T(8,128)(2,1)} %copy.58) | copy-start | bytes 6488068
  724.5 17.2 %copy-start.11 = (f32[384,32]{0,1:T(8,128)S(1)}, f32[384,32]{0,1:T(8,128)}, u32[]{:S(2)}) copy-start(f32[384,32]{0,1:T(8,128)} %param.12) | copy-start | bytes 147460
  (3 other events, 5.8 us)
Sparse Core Ops, SparseCore 0:
  401.8 188.2 all-reduce.3
